TPU v7x, 32 devices: a whole 2x2x4 slice. The times are simulated.
32 devices in a mesh: parts: 2 (over y), holder: 4 (over x, core), query: 4 (over z).
Axes of the slice: x: 2, y: 2, z: 4, core: 2. Of those that a mesh axis runs over, the one named last changes fastest.
Arguments:
- queries: bfloat16 [32, 32, 128], P(('parts', 'holder', 'query')), parts along dimension 0, may hold values from -6 to 6
- candidates: int32 [32, 256], P(('parts', 'holder', 'query')), parts along dimension 0, may hold values from 0 to 511, all different within a row; in each aligned block of 16 rows (0 to 15, 16 to 31, ...) at most 16 rows name the same one
- page_slot: int32 [1024], P('parts'), parts along dimension 0, may hold values from 0 to 511, each once
- page_embeddings: bfloat16 [1024, 1024, 128], P(('parts', 'holder'), 'query'), parts along dimension 0, may hold values from -0.5 to 0.5
Outputs:
- scores: float32 [32, 256], P(('parts', 'holder', 'query')), parts along dimension 0
There are 2 independent parts, one for each index of `parts`. A program takes and returns all parts, laid end to end along the dimension named above; each array names one. Nothing has to cross between parts.
Inputs may be any that keep to these rules, and one draw needn't show every extreme that they name: `candidates`: each row names 256 different pages; no page is named by more than 16 rows, a bound that some block reaches. A permutation: page id p is stored at row page_slot[p] of page_embeddings.
All inputs are finite; a program needn't handle non-finite values.
Results may differ from a plain program's by a relative error of at most 0.0003.
Values may be sent and summed in bfloat16 or wider, within the bound.
A program may use at most 64 MiB of HBM per device.

v0:
```python
import math

import jax
import jax.numpy as jnp
from jax import lax
from jax.sharding import PartitionSpec as P

MOST = 32


def build_table(pair_score, placed, local_row, first_row, row_count):
    picked = lax.dynamic_slice_in_dim(placed, first_row, row_count, 1)
    per_page = jnp.sum(jnp.where(picked, pair_score[None, :, :], 0.0), axis=2)
    offset = local_row - first_row
    inside = (offset >= 0) & (offset < row_count)
    clipped = jnp.clip(offset, 0, row_count - 1)
    values = jnp.take_along_axis(per_page, clipped, axis=1)
    return jnp.where(inside, values, 0.0)


def shards(queries, candidates, page_slot, page_embeddings):
    askers = lax.axis_size("query")
    gathered, wanted = (
        lax.all_gather(queries, ("holder", "query"), axis=0, tiled=True),
        lax.all_gather(candidates, ("holder", "query"), axis=0, tiled=True),
    )
    all_queries = gathered.shape[0]
    tokens_per = gathered.shape[1]
    local_pages = page_embeddings.shape[0]
    capacity = min(MOST, all_queries)
    holder_id = lax.axis_index("holder")
    stored = jnp.take(page_slot, wanted, axis=0)
    mine = stored // local_pages == holder_id
    local_row = jnp.where(mine, stored % local_pages, local_pages)
    page_ids = jnp.arange(local_pages, dtype=jnp.int32)
    hit_table = jnp.any(local_row[:, :, None] == page_ids[None, None, :], axis=1).astype(jnp.int32)
    before = jnp.cumsum(hit_table, axis=0) - hit_table
    slot_ids = jnp.arange(capacity, dtype=jnp.int32)
    placed = (hit_table[:, :, None] == 1) & (before[:, :, None] == slot_ids[None, None, :])
    asker_ids = jnp.arange(all_queries, dtype=jnp.int32)
    slot_query = jnp.sum(jnp.where(placed, asker_ids[:, None, None], 0), axis=0)
    block_size = math.gcd(local_pages, 8)
    blocks = local_pages // block_size
    page_blocks = page_embeddings.reshape((blocks, block_size) + page_embeddings.shape[1:])
    slot_blocks = slot_query.reshape(blocks, block_size, capacity)

    def block_max(inputs):
        page_block, slot_block = inputs
        chosen = jnp.take(gathered, slot_block, axis=0)
        products = jnp.einsum(
            "bcte,bpe->bctp", chosen, page_block, preferred_element_type=jnp.float32
        )
        return jnp.max(products, axis=3).reshape(block_size, capacity * tokens_per)

    maxima = lax.map(block_max, (page_blocks, slot_blocks)).reshape(
        local_pages, capacity * tokens_per
    )
    asker_id = lax.axis_index("query")
    share_rows = local_pages // askers
    arrived = lax.all_to_all(
        maxima.reshape(1, local_pages, capacity * tokens_per),
        "query",
        split_axis=1,
        concat_axis=0,
        tiled=True,
    )
    share_max = jnp.max(arrived, axis=0)
    pair_score = jnp.sum(share_max.reshape(share_rows, capacity, tokens_per), axis=2) / tokens_per
    first_row = asker_id * share_rows
    score_table = build_table(pair_score, placed, local_row, first_row, share_rows)
    result = lax.psum_scatter(score_table, ("holder", "query"), scatter_dimension=0, tiled=True)
    return result


def solution(mesh):
    placed = (
        P(("parts", "holder", "query"), None, None),
        P(("parts", "holder", "query"), None),
        P("parts"),
        P(("parts", "holder"), "query", None),
    )
    return jax.shard_map(
        shards,
        mesh=mesh,
        in_specs=placed,
        out_specs=P(("parts", "holder", "query"), None),
        check_vma=False,
    )
```

profile of v0, /device:TPU:0, one launch (start us, length us, event | category | flops | bytes accessed | tf_op | source)
XLA Modules:
  0.0 235.9 jit_solution(15723160992976962355)
XLA Ops:
  0.0 34.2 %all-gather = s32[16,1,256]{2,1,0:T(1,128)S(1)} all-gather(s32[1,1,256]{2,1,0:T(1,128)} %bitcast.51), channel_id=1, replica_groups=mesh['parts'=2,'holder'=4,'query'=4] {'holder','query'}, dimensions={0}, use_global_device_ids=true | all-gather | bytes 17408 | tf_op jit(solution)/shard_map/all_gather | solution.py:25
  34.3 25.8 %gather_fusion.1 = s32[4096]{0:T(1024)S(1)} fusion(s32[512]{0:T(512)S(1)} %copy-done, s32[4096]{0:T(1024)S(1)} %broadcast_clamp_fusion), kind=kCustom, calls=%fused_computation.1 | custom fusion | bytes 49152 | tf_op jit(solution)/shard_map/jit(_take)/gather | solution.py:32
  60.2 0.7 fusion.7
  61.0 0.1 copy.9
  61.1 29.5 %all_gather.7 = bf16[16,32,128]{2,1,0:T(8,128)(2,1)S(1)} all-gather(bf16[1,32,128]{2,1,0:T(8,128)(2,1)S(1)} %copy-done.1), channel_id=1, replica_groups=mesh['parts'=2,'holder'=4,'query'=4] {'holder','query'}, dimensions={0}, use_global_device_ids=true | all-gather | bytes 139264 | tf_op jit(solution)/shard_map/all_gather | solution.py:24
  90.6 46.4 %while.10 = (s32[]{:T(128)}, f32[16,8,512]{2,1,0:T(8,128)S(1)}, s32[16,8,16]{2,1,0:T(8,128)S(1)}, bf16[16,32,128]{2,1,0:T(8,128)(2,1)S(1)}, bf16[16,8,256,128]{3,2,1,0:T(8,128)(2,1)}, /*index=5*/s32[]{:T(128)}) while((s32[]{:T(128)}, f32[16,8,512]{2,1,0:T(8,128)S(1)}, s32[16,8,16]{2,1,0:T(8,128)S(1)}, bf16[16,32,128]{2,1,0:T(8,128)(2,1)S(1)}, ...), condition=%wide.region_5.6_spmd, body=%wide.region_3.5_spmd.sunk | while | flops 270006400 | bytes 3760465 | solution.py:55
  90.7 0.8 gather_fusion
  91.5 1.9 convolution_reduce_fusion.2
  93.6 0.8 gather_fusion
  94.4 1.9 convolution_reduce_fusion.2
  96.5 0.8 gather_fusion
  97.3 1.9 convolution_reduce_fusion.2
  99.4 0.8 gather_fusion
  100.2 1.9 convolution_reduce_fusion.2
  102.3 0.8 gather_fusion
  103.1 1.9 convolution_reduce_fusion.2
  105.2 0.8 gather_fusion
  106.0 1.9 convolution_reduce_fusion.2
  108.1 0.8 gather_fusion
  108.9 1.9 convolution_reduce_fusion.2
  111.0 0.8 gather_fusion
  111.8 1.9 convolution_reduce_fusion.2
  113.9 0.8 gather_fusion
  114.7 1.9 convolution_reduce_fusion.2
  116.8 0.8 gather_fusion
  117.6 1.9 convolution_reduce_fusion.2
  119.7 0.8 gather_fusion
  120.5 1.9 convolution_reduce_fusion.2
  122.6 0.8 gather_fusion
  123.4 1.9 convolution_reduce_fusion.2
  125.5 0.8 gather_fusion
  126.3 1.9 convolution_reduce_fusion.2
  128.4 0.8 gather_fusion
  129.2 1.9 convolution_reduce_fusion.2
  131.3 0.8 gather_fusion
  132.1 1.9 convolution_reduce_fusion.2
  134.2 0.8 gather_fusion
  135.0 1.9 convolution_reduce_fusion.2
  137.0 1.0 reshape_reshape.3
  138.0 3.4 %all-to-all-start = ((f32[1,128,512]{2,0,1:T(1,128)}), f32[1,128,512]{2,0,1:T(1,128)S(1)}, u32[]{:S(2)}, u32[]{:S(2)}) async-start(f32[1,128,512]{2,0,1:T(1,128)} %reshape_reshape.3), calls=%async_computation | async-start | bytes 524288 | tf_op jit(solution)/shard_map/all_to_all | solution.py:60
  141.4 0.6 dynamic-slice
  142.1 6.1 %all-to-all-done = f32[1,128,512]{2,0,1:T(1,128)S(1)} async-done(((f32[1,128,512]{2,0,1:T(1,128)}), f32[1,128,512]{2,0,1:T(1,128)S(1)}, u32[]{:S(2)}, u32[]{:S(2)}) %all-to-all-start) | async-done | bytes 262176 | tf_op jit(solution)/shard_map/all_to_all | solution.py:60
  148.2 0.1 reshape.118
  148.3 0.1 reduce_sum.28
  148.6 0.1 select_reduce_fusion
  148.7 26.7 %gather_fusion.2 = f32[4096]{0:T(1024)S(1)} fusion(f32[16,32]{1,0:T(8,128)S(1)} %select_reduce_fusion, s32[4096]{0:T(1024)S(1)} %bitcast.46), kind=kCustom, calls=%fused_computation.2 | custom fusion | bytes 65536 | tf_op jit(solution)/shard_map/jit(take_along_axis)/gather | solution.py:17
  175.4 59.3 %all-reduce = f32[16,256]{1,0:T(8,128)S(1)} all-reduce(f32[16,256]{1,0:T(8,128)S(1)} %select_select_fusion), channel_id=2, replica_groups=mesh['parts'=2,'holder'=4,'query'=4] {'holder','query'}, use_global_device_ids=true, to_apply=%region_9.10.clone | all-reduce | flops 4096 | bytes 32768
  234.7 1.2 constant_dynamic-slice_fusion
  (120 shorter events, 3.7 us)
Async XLA Ops:
  0.0 34.3 %copy-start = (s32[512]{0:T(512)S(1)}, s32[512]{0:T(512)}, u32[]{:S(2)}) copy-start(s32[512]{0:T(512)} %param.8) | copy-start | bytes 6148
  34.3 26.8 %copy-start.1 = (bf16[1,32,128]{2,1,0:T(8,128)(2,1)S(1)}, bf16[1,32,128]{2,1,0:T(8,128)(2,1)}, u32[]{:S(2)}) copy-start(bf16[1,32,128]{2,1,0:T(8,128)(2,1)} %param.6) | copy-start | bytes 24580
  90.6 50.8 %copy-start.2 = (u32[32]{0:T(128)S(1)}, u32[32]{0:T(128)}, u32[]{:S(2)}) copy-start(u32[32]{0:T(128)} %constant.131) | copy-start | bytes 388
  138.0 10.2 %all-to-all-start = ((f32[1,128,512]{2,0,1:T(1,128)}), f32[1,128,512]{2,0,1:T(1,128)S(1)}, u32[]{:S(2)}, u32[]{:S(2)}) async-start(f32[1,128,512]{2,0,1:T(1,128)} %reshape_reshape.3), calls=%async_computation | async-start | bytes 524288 | tf_op jit(solution)/shard_map/all_to_all | solution.py:60
where the time goes:
time: 237 us; the launch traced here: 236 us
  blocking collectives  123 us (52%)
  local copies, waits for them, and re-layouts  70.6 us (30%)
  matrix products  30.2 us (13%)
  waiting for transfers between devices  6.07 us (3%)
  starting transfers between devices  3.42 us (1%)
    unnamed x1, blocking collectives  59.3 us
    all_gather x1, blocking collectives, shards(): lax.all_gather(candidates, ('holder', 'query'), axis=0, tiled=True)  34.2 us
    dot_general x16, matrix products, block_max(): jnp.einsum('bcte,bpe->bctp', chosen, page_block, preferred_element_type=j...  30.2 us
    all_gather x1, blocking collectives, shards(): lax.all_gather(queries, ('holder', 'query'), axis=0, tiled=True)  29.5 us
    gather x2, local copies, waits for them, and re-layouts, build_table(): values = jnp.take_along_axis(per_page, clipped, axis=1)  26.7 us
    gather x2, local copies, waits for them, and re-layouts, shards(): stored = jnp.take(page_slot, wanted, axis=0)  25.9 us
    gather x16, local copies, waits for them, and re-layouts, block_max(): chosen = jnp.take(gathered, slot_block, axis=0)  12.1 us
    all_to_all x1, waiting for transfers between devices, shards(): lax.all_to_all(maxima.reshape(1, local_pages, capacity * tokens_per), 'qu...  6.07 us
  transfers between devices with their start and end apart: 1, of which 1 were waited for; matrix products, arithmetic and copies ran while one was open for 0% of the time, Pallas kernels for 0%

commit v1 on v0

v1 whole, which is shorter than its diff:
```python
import functools

import jax
import jax.numpy as jnp
from jax import lax
from jax.experimental import pallas as pl
from jax.experimental.pallas import tpu as pltpu
from jax.sharding import PartitionSpec as P

MESH = pl.DeviceIdType.MESH
WIDE = 256
GROUP = 8
BLOCKS = 4
NT = (((1,), (1,)), ((), ()))
NN = (((1,), (0,)), ((), ()))


def split3(x):
    high = x.astype(jnp.bfloat16)
    rest = x - high.astype(jnp.float32)
    mid = rest.astype(jnp.bfloat16)
    low = (rest - mid.astype(jnp.float32)).astype(jnp.bfloat16)
    return high, mid, low


def dot(a, b, dims):
    return lax.dot_general(a, b, dims, preferred_element_type=jnp.float32)


def kernel(
    holders, askers, q_ref, cand_ref, slot_ref, emb_ref, out_ref,
    pages, qbuf, best, arrived, row, table,
    load_sem, qz_sem, qh_sem, qr_sem, ms_sem, mr_sem, ss_sem, sr_sem,
):
    h = lax.axis_index("holder")
    z = lax.axis_index("query")
    tokens = q_ref.shape[1]
    count, patches, width = pages.shape
    cols = holders * tokens
    block = count // BLOCKS
    z_peers = [lax.rem(z + d, askers) for d in range(1, askers)]
    h_peers = [lax.rem(h + d, holders) for d in range(1, holders)]

    loads = []
    for b in range(BLOCKS):
        part = pl.ds(b * block, block)
        load = pltpu.make_async_copy(emb_ref.at[part], pages.at[part], load_sem.at[b])
        load.start()
        loads.append(load)

    barrier = pltpu.get_barrier_semaphore()
    for peer in z_peers:
        pl.semaphore_signal(barrier, inc=1, device_id={"query": peer}, device_id_type=MESH)
    for peer in h_peers:
        pl.semaphore_signal(barrier, inc=1, device_id={"holder": peer}, device_id_type=MESH)

    slots = slot_ref[...]
    slot_rows = jnp.concatenate([slots // count, slots % count] + [jnp.zeros_like(slots)] * 6, axis=0)
    wanted = cand_ref[...]
    pages_in_all = slots.shape[1]
    ids = lax.broadcasted_iota(jnp.int32, (pages_in_all, wanted.shape[1]), 0)
    is_page = (ids == wanted).astype(jnp.float32).astype(jnp.bfloat16)
    place = dot(slot_rows.astype(jnp.float32).astype(jnp.bfloat16), is_page, NN)
    at_holder = place[0:1].astype(jnp.int32)
    at_row = place[1:2].astype(jnp.int32)
    row_ids = lax.broadcasted_iota(jnp.int32, (count, wanted.shape[1]), 0)
    is_row = (row_ids == at_row).astype(jnp.float32).astype(jnp.bfloat16)

    own = pl.ds(pl.multiple_of(h * tokens, tokens), tokens)
    qbuf[z, own, :] = q_ref[0]
    pl.semaphore_wait(barrier, askers + holders - 2)

    sends = []
    for peer in z_peers:
        copy = pltpu.make_async_remote_copy(
            src_ref=q_ref.at[0], dst_ref=qbuf.at[z, own], send_sem=qz_sem.at[peer],
            recv_sem=qr_sem.at[z, h], device_id={"query": peer}, device_id_type=MESH,
        )
        copy.start()
        sends.append(copy)

    def forward(at, src):
        for peer in h_peers:
            copy = pltpu.make_async_remote_copy(
                src_ref=src, dst_ref=qbuf.at[at, own], send_sem=qh_sem.at[at, peer],
                recv_sem=qr_sem.at[at, h], device_id={"holder": peer}, device_id_type=MESH,
            )
            copy.start()
            sends.append(copy)

    def await_query(at, who):
        rows = pl.ds(pl.multiple_of(who * tokens, tokens), tokens)
        pltpu.make_async_copy(qbuf.at[at, rows], qbuf.at[at, rows], qr_sem.at[at, who]).wait()

    forward(z, q_ref.at[0])
    for peer in z_peers:
        await_query(peer, h)
        forward(peer, qbuf.at[peer, own])

    together = max(1, WIDE // cols)
    if askers % together:
        together = 1
    rounds = askers // together
    mine = z // together
    for i in range(rounds):
        chunk = lax.rem(mine + 1 + i, rounds)
        first = chunk * together
        if i == rounds - 1:
            members = [first + lax.rem(lax.rem(z, together) + j, together) for j in range(together)]
            others = members[1:]
        else:
            members = [first + j for j in range(together)]
            others = members
        for at in members:
            for peer in h_peers:
                await_query(at, peer)
        for b in range(BLOCKS):
            if i == 0:
                loads[b].wait()

            def step(g, carry):
                start = pl.multiple_of(b * block + g * GROUP, GROUP)
                tall = pages[pl.ds(start, GROUP)].reshape(GROUP * patches, width)
                tok = qbuf[pl.ds(first, together)].reshape(together * cols, width)
                sims = dot(tall, tok, NT).reshape(GROUP, patches, together * cols)
                top = jnp.max(sims, axis=1)
                for j in range(together):
                    best[first + j, pl.ds(start, GROUP), :] = top[:, j * cols : (j + 1) * cols]
                return carry

            lax.fori_loop(0, block // GROUP, step, 0)
            part = pl.ds(b * block, block)
            for at in others:
                copy = pltpu.make_async_remote_copy(
                    src_ref=best.at[at, part], dst_ref=arrived.at[z, part], send_sem=ms_sem.at[at, b],
                    recv_sem=mr_sem.at[z, b], device_id={"query": at}, device_id_type=MESH,
                )
                copy.start()
                sends.append(copy)

    parts = []
    for b in range(BLOCKS):
        part = pl.ds(b * block, block)
        top = best[z, part, :]
        for peer in z_peers:
            pltpu.make_async_copy(arrived.at[peer, part], arrived.at[peer, part], mr_sem.at[peer, b]).wait()
            top = jnp.maximum(top, arrived[peer, part, :])
        parts.append(top)
    top = jnp.concatenate(parts, axis=0)
    tall = -(-holders // 8) * 8
    owner = lax.broadcasted_iota(jnp.int32, (tall, cols), 0)
    column = lax.broadcasted_iota(jnp.int32, (tall, cols), 1)
    low = owner * tokens
    member = ((column >= low) & (column < low + tokens)).astype(jnp.float32).astype(jnp.bfloat16)
    high, mid, rest = split3(top)
    scores = (dot(member, high, NT) + dot(member, mid, NT) + dot(member, rest, NT)) * (1.0 / tokens)
    for k in range(holders):
        row[k] = scores[k : k + 1]
    for peer in h_peers:
        copy = pltpu.make_async_remote_copy(
            src_ref=row.at[peer], dst_ref=table.at[h], send_sem=ss_sem.at[peer],
            recv_sem=sr_sem.at[h], device_id={"holder": peer}, device_id_type=MESH,
        )
        copy.start()
        sends.append(copy)
    table[h] = row[h]
    for peer in h_peers:
        pltpu.make_async_copy(table.at[peer], table.at[peer], sr_sem.at[peer]).wait()

    known = [table[k] for k in range(holders)]
    known = jnp.concatenate(known + [jnp.zeros_like(known[0])] * (tall - holders), axis=0)
    high, mid, rest = split3(known)
    found = dot(high, is_row, NN) + dot(mid, is_row, NN) + dot(rest, is_row, NN)
    holder_ids = lax.broadcasted_iota(jnp.int32, found.shape, 0)
    out_ref[...] = jnp.sum(jnp.where(holder_ids == at_holder, found, 0.0), axis=0, keepdims=True)
    for copy in sends:
        copy.wait_send()


def shards(holders, askers, queries, candidates, page_slot, page_embeddings):
    _, tokens, width = queries.shape
    count, patches, _ = page_embeddings.shape
    cols = holders * tokens
    vmem = pl.BlockSpec(memory_space=pltpu.VMEM)
    dma = pltpu.SemaphoreType.DMA
    return pl.pallas_call(
        functools.partial(kernel, holders, askers),
        out_shape=jax.ShapeDtypeStruct(candidates.shape, jnp.float32),
        in_specs=[vmem, vmem, vmem, pl.BlockSpec(memory_space=pl.ANY)],
        out_specs=vmem,
        scratch_shapes=[
            pltpu.VMEM((count, patches, width), jnp.bfloat16),
            pltpu.VMEM((askers, cols, width), jnp.bfloat16),
            pltpu.VMEM((askers, count, cols), jnp.float32),
            pltpu.VMEM((askers, count, cols), jnp.float32),
            pltpu.VMEM((holders, 1, count), jnp.float32),
            pltpu.VMEM((holders, 1, count), jnp.float32),
            dma((BLOCKS,)),
            dma((askers,)),
            dma((askers, holders)),
            dma((askers, holders)),
            dma((askers, BLOCKS)),
            dma((askers, BLOCKS)),
            dma((holders,)),
            dma((holders,)),
        ],
        compiler_params=pltpu.CompilerParams(
            collective_id=0, has_side_effects=True, vmem_limit_bytes=48 * 1024 * 1024
        ),
    )(queries, candidates, page_slot.reshape(1, -1), page_embeddings)


def solution(mesh):
    placed = (
        P(("parts", "holder", "query"), None, None),
        P(("parts", "holder", "query"), None),
        P("parts"),
        P(("parts", "holder"), "query", None),
    )
    return jax.shard_map(
        functools.partial(shards, mesh.shape["holder"], mesh.shape["query"]),
        mesh=mesh,
        in_specs=placed,
        out_specs=P(("parts", "holder", "query"), None),
        check_vma=False,
    )
```

time: 237 us -> 33.9 us (0.14)
  blocking collectives: 123 us -> 0 us
  local copies, waits for them, and re-layouts: 70.6 us -> 2.62 us
  Pallas kernels: 0 us -> 31 us
  matrix products: 30.2 us -> 0 us
  waiting for transfers between devices: 6.07 us -> 0 us
  starting transfers between devices: 3.42 us -> 0 us
    gather x20 -> x0, local copies, waits for them, and re-layouts: 64.6 us -> none  [the longest x2 26.7 us: build_table(): values = jnp.take_along_axis(per_page, clipped, axis=1)]
    all_gather x2 -> x0, blocking collectives: 63.7 us -> none  [the longest x1 34.2 us: shards(): lax.all_gather(candidates, ('holder', 'query'), axis=0, tiled=True)]
    unnamed x1 -> x0, blocking collectives: 59.3 us -> none
    pallas_call x0 -> x1, Pallas kernels: none -> 31 us  [shards(): pl.pallas_call(functools.partial(kernel, holders, askers), out_shape=jax....]
    dot_general x16 -> x0, matrix products: 30.2 us -> none  [block_max(): jnp.einsum('bcte,bpe->bctp', chosen, page_block, preferred_element_type=j...]
    all_to_all x1 -> x0, waiting for transfers between devices: 6.07 us -> none  [shards(): lax.all_to_all(maxima.reshape(1, local_pages, capacity * tokens_per), 'qu...]
    all_to_all x1 -> x0, starting transfers between devices: 3.42 us -> none  [shards(): lax.all_to_all(maxima.reshape(1, local_pages, capacity * tokens_per), 'qu...]
  transfers between devices with their start and end apart: 1 -> 0, of which waited for: 1 -> 0; matrix products, arithmetic and copies ran while one was open for 0% -> 0% of each run, Pallas kernels for 0% -> 0%
where the time goes in v1:
time: 33.9 us; the launch traced here: 33.7 us
  Pallas kernels  31 us (91%)
  local copies, waits for them, and re-layouts  2.62 us (8%)
    pallas_call x1, Pallas kernels, shards(): pl.pallas_call(functools.partial(kernel, holders, askers), out_shape=jax....  31 us
    unnamed x7, local copies, waits for them, and re-layouts  2.62 us

profile of v1, /device:TPU:0, one launch (start us, length us, event | category | flops | bytes accessed | tf_op | source)
XLA Modules:
  0.0 33.7 jit_solution(9316896148246656413)
XLA Ops:
  0.0 0.0 copy-start
  0.0 0.7 %copy-done = bf16[1,32,128]{2,1,0:T(8,128)(2,1)S(1)} copy-done((bf16[1,32,128]{2,1,0:T(8,128)(2,1)S(1)}, bf16[1,32,128]{2,1,0:T(8,128)(2,1)}, u32[]{:S(2)}) %copy-start) | copy-done | bytes 8216
  0.7 0.0 copy-start.1
  0.7 0.7 %copy-done.1 = s32[512]{0:T(512)S(1)} copy-done((s32[512]{0:T(512)S(1)}, s32[512]{0:T(512)}, u32[]{:S(2)}) %copy-start.1) | copy-done | bytes 2072
  1.4 0.0 copy-start.2
  1.4 0.7 %copy-done.2 = s32[1,256]{1,0:T(1,128)S(1)} copy-done((s32[1,256]{1,0:T(1,128)S(1)}, s32[1,256]{1,0:T(1,128)}, u32[]{:S(2)}) %copy-start.2) | copy-done | bytes 1048
  2.1 31.0 %shard_map.46 = f32[1,256]{1,0:T(1,128)S(1)} custom-call(bf16[1,32,128]{2,1,0:T(8,128)(2,1)S(1)} %copy-done, s32[1,256]{1,0:T(1,128)S(1)} %copy-done.2, s32[1,512]{1,0:T(1,128)S(1)} %bitcast.1, bf16[128,256,128]{2,1,0:T(8,128)(2,1)} %emb_ref.1), custom_call_target="tpu_custom_call" | custom-call | tf_op jit(solution)/shard_map/pallas_call | solution.py:186
  33.1 0.6 %copy.6 = f32[1,256]{1,0:T(1,128)} copy(f32[1,256]{1,0:T(1,128)S(1)} %shard_map.46) | data formatting | bytes 2048
Async XLA Ops:
  0.0 0.7 %copy-start = (bf16[1,32,128]{2,1,0:T(8,128)(2,1)S(1)}, bf16[1,32,128]{2,1,0:T(8,128)(2,1)}, u32[]{:S(2)}) copy-start(bf16[1,32,128]{2,1,0:T(8,128)(2,1)} %q_ref.1) | copy-start | bytes 24580
  0.7 0.7 %copy-start.1 = (s32[512]{0:T(512)S(1)}, s32[512]{0:T(512)}, u32[]{:S(2)}) copy-start(s32[512]{0:T(512)} %param.6) | copy-start | bytes 6148
  1.4 0.7 %copy-start.2 = (s32[1,256]{1,0:T(1,128)S(1)}, s32[1,256]{1,0:T(1,128)}, u32[]{:S(2)}) copy-start(s32[1,256]{1,0:T(1,128)} %cand_ref.1) | copy-start | bytes 3076

commit v2 on v1

--- a/solution.py
+++ b/solution.py
@@ -9,7 +9,6 @@
 
 MESH = pl.DeviceIdType.MESH
 WIDE = 256
-GROUP = 8
 BLOCKS = 4
 NT = (((1,), (1,)), ((), ()))
 NN = (((1,), (0,)), ((), ()))
@@ -29,8 +28,8 @@
 
 def kernel(
     holders, askers, q_ref, cand_ref, slot_ref, emb_ref, out_ref,
-    pages, qbuf, best, arrived, row, table,
-    load_sem, qz_sem, qh_sem, qr_sem, ms_sem, mr_sem, ss_sem, sr_sem,
+    pages, qbuf, best, arrived, row, table, cand, slot,
+    load_sem, own_sem, in_sem, qz_sem, qh_sem, qr_sem, ms_sem, mr_sem, ss_sem, sr_sem,
 ):
     h = lax.axis_index("holder")
     z = lax.axis_index("query")
@@ -41,12 +40,24 @@
     z_peers = [lax.rem(z + d, askers) for d in range(1, askers)]
     h_peers = [lax.rem(h + d, holders) for d in range(1, holders)]
 
-    loads = []
+    own = pl.ds(pl.multiple_of(h * tokens, tokens), tokens)
+    keep = pltpu.make_async_copy(q_ref.at[0], qbuf.at[z, own], own_sem)
+    keep.start()
+    small = [
+        pltpu.make_async_copy(slot_ref, slot, in_sem.at[0]),
+        pltpu.make_async_copy(cand_ref, cand, in_sem.at[1]),
+    ]
+    for copy in small:
+        copy.start()
+
+    def block_of(b):
+        return pl.ds(pl.multiple_of(b * block, block), block)
+
+    def load(b):
+        return pltpu.make_async_copy(emb_ref.at[block_of(b)], pages.at[block_of(b)], load_sem.at[b])
+
     for b in range(BLOCKS):
-        part = pl.ds(b * block, block)
-        load = pltpu.make_async_copy(emb_ref.at[part], pages.at[part], load_sem.at[b])
-        load.start()
-        loads.append(load)
+        load(b).start()
 
     barrier = pltpu.get_barrier_semaphore()
     for peer in z_peers:
@@ -54,9 +65,37 @@
     for peer in h_peers:
         pl.semaphore_signal(barrier, inc=1, device_id={"holder": peer}, device_id_type=MESH)
 
-    slots = slot_ref[...]
+    pl.semaphore_wait(barrier, askers + holders - 2)
+
+    sends = []
+    for peer in z_peers:
+        copy = pltpu.make_async_remote_copy(
+            src_ref=q_ref.at[0], dst_ref=qbuf.at[z, own], send_sem=qz_sem.at[peer],
+            recv_sem=qr_sem.at[z, h], device_id={"query": peer}, device_id_type=MESH,
+        )
+        copy.start()
+        sends.append(copy)
+
+    def forward(at, src):
+        for peer in h_peers:
+            copy = pltpu.make_async_remote_copy(
+                src_ref=src, dst_ref=qbuf.at[at, own], send_sem=qh_sem.at[at, peer],
+                recv_sem=qr_sem.at[at, h], device_id={"holder": peer}, device_id_type=MESH,
+            )
+            copy.start()
+            sends.append(copy)
+
+    def await_query(at, who):
+        rows = pl.ds(pl.multiple_of(who * tokens, tokens), tokens)
+        pltpu.make_async_copy(qbuf.at[at, rows], qbuf.at[at, rows], qr_sem.at[at, who]).wait()
+
+    forward(z, q_ref.at[0])
+
+    for copy in small:
+        copy.wait()
+    slots = slot[...]
     slot_rows = jnp.concatenate([slots // count, slots % count] + [jnp.zeros_like(slots)] * 6, axis=0)
-    wanted = cand_ref[...]
+    wanted = cand[...]
     pages_in_all = slots.shape[1]
     ids = lax.broadcasted_iota(jnp.int32, (pages_in_all, wanted.shape[1]), 0)
     is_page = (ids == wanted).astype(jnp.float32).astype(jnp.bfloat16)
@@ -66,33 +105,7 @@
     row_ids = lax.broadcasted_iota(jnp.int32, (count, wanted.shape[1]), 0)
     is_row = (row_ids == at_row).astype(jnp.float32).astype(jnp.bfloat16)
 
-    own = pl.ds(pl.multiple_of(h * tokens, tokens), tokens)
-    qbuf[z, own, :] = q_ref[0]
-    pl.semaphore_wait(barrier, askers + holders - 2)
-
-    sends = []
-    for peer in z_peers:
-        copy = pltpu.make_async_remote_copy(
-            src_ref=q_ref.at[0], dst_ref=qbuf.at[z, own], send_sem=qz_sem.at[peer],
-            recv_sem=qr_sem.at[z, h], device_id={"query": peer}, device_id_type=MESH,
-        )
-        copy.start()
-        sends.append(copy)
-
-    def forward(at, src):
-        for peer in h_peers:
-            copy = pltpu.make_async_remote_copy(
-                src_ref=src, dst_ref=qbuf.at[at, own], send_sem=qh_sem.at[at, peer],
-                recv_sem=qr_sem.at[at, h], device_id={"holder": peer}, device_id_type=MESH,
-            )
-            copy.start()
-            sends.append(copy)
-
-    def await_query(at, who):
-        rows = pl.ds(pl.multiple_of(who * tokens, tokens), tokens)
-        pltpu.make_async_copy(qbuf.at[at, rows], qbuf.at[at, rows], qr_sem.at[at, who]).wait()
-
-    forward(z, q_ref.at[0])
+    keep.wait()
     for peer in z_peers:
         await_query(peer, h)
         forward(peer, qbuf.at[peer, own])
@@ -101,6 +114,13 @@
     if askers % together:
         together = 1
     rounds = askers // together
+
+    def hand_over(at, b):
+        return pltpu.make_async_remote_copy(
+            src_ref=best.at[at, block_of(b)], dst_ref=arrived.at[z, block_of(b)], send_sem=ms_sem.at[at, b],
+            recv_sem=mr_sem.at[z, b], device_id={"query": at}, device_id_type=MESH,
+        )
+
     mine = z // together
     for i in range(rounds):
         chunk = lax.rem(mine + 1 + i, rounds)
@@ -114,29 +134,22 @@
         for at in members:
             for peer in h_peers:
                 await_query(at, peer)
-        for b in range(BLOCKS):
+
+        def work(b, carry):
             if i == 0:
-                loads[b].wait()
-
-            def step(g, carry):
-                start = pl.multiple_of(b * block + g * GROUP, GROUP)
-                tall = pages[pl.ds(start, GROUP)].reshape(GROUP * patches, width)
-                tok = qbuf[pl.ds(first, together)].reshape(together * cols, width)
-                sims = dot(tall, tok, NT).reshape(GROUP, patches, together * cols)
-                top = jnp.max(sims, axis=1)
-                for j in range(together):
-                    best[first + j, pl.ds(start, GROUP), :] = top[:, j * cols : (j + 1) * cols]
-                return carry
-
-            lax.fori_loop(0, block // GROUP, step, 0)
-            part = pl.ds(b * block, block)
+                load(b).wait()
+            part = block_of(b)
+            tall = pages[part].reshape(block * patches, width)
+            tok = qbuf[pl.ds(first, together)].reshape(together * cols, width)
+            sims = dot(tall, tok, NT).reshape(block, patches, together * cols)
+            top = jnp.max(sims, axis=1)
+            for j in range(together):
+                best[first + j, part, :] = top[:, j * cols : (j + 1) * cols]
             for at in others:
-                copy = pltpu.make_async_remote_copy(
-                    src_ref=best.at[at, part], dst_ref=arrived.at[z, part], send_sem=ms_sem.at[at, b],
-                    recv_sem=mr_sem.at[z, b], device_id={"query": at}, device_id_type=MESH,
-                )
-                copy.start()
-                sends.append(copy)
+                hand_over(at, b).start()
+            return carry
+
+        lax.fori_loop(0, BLOCKS, work, 0)
 
     parts = []
     for b in range(BLOCKS):
@@ -175,6 +188,9 @@
     out_ref[...] = jnp.sum(jnp.where(holder_ids == at_holder, found, 0.0), axis=0, keepdims=True)
     for copy in sends:
         copy.wait_send()
+    for peer in z_peers:
+        for b in range(BLOCKS):
+            hand_over(peer, b).wait_send()
 
 
 def shards(holders, askers, queries, candidates, page_slot, page_embeddings):
@@ -186,7 +202,7 @@
     return pl.pallas_call(
         functools.partial(kernel, holders, askers),
         out_shape=jax.ShapeDtypeStruct(candidates.shape, jnp.float32),
-        in_specs=[vmem, vmem, vmem, pl.BlockSpec(memory_space=pl.ANY)],
+        in_specs=[pl.BlockSpec(memory_space=pl.ANY)] * 4,
         out_specs=vmem,
         scratch_shapes=[
             pltpu.VMEM((count, patches, width), jnp.bfloat16),
@@ -195,7 +211,11 @@
             pltpu.VMEM((askers, count, cols), jnp.float32),
             pltpu.VMEM((holders, 1, count), jnp.float32),
             pltpu.VMEM((holders, 1, count), jnp.float32),
+            pltpu.VMEM(candidates.shape, jnp.int32),
+            pltpu.VMEM((1, page_slot.shape[0]), jnp.int32),
             dma((BLOCKS,)),
+            dma,
+            dma((2,)),
             dma((askers,)),
             dma((askers, holders)),
             dma((askers, holders)),
@@ -205,7 +225,7 @@
             dma((holders,)),
         ],
         compiler_params=pltpu.CompilerParams(
-            collective_id=0, has_side_effects=True, vmem_limit_bytes=48 * 1024 * 1024
+            collective_id=0, has_side_effects=True, vmem_limit_bytes=64 * 1024 * 1024
         ),
     )(queries, candidates, page_slot.reshape(1, -1), page_embeddings)
 

time: 33.9 us -> 29.2 us (0.86)
  Pallas kernels: 31 us -> 27.8 us
  local copies, waits for them, and re-layouts: 2.62 us -> 1.24 us
    pallas_call x1, Pallas kernels: 31 us -> 27.8 us  [shards(): pl.pallas_call(functools.partial(kernel, holders, askers), out_shape=jax....]
    unnamed x7 -> x1, local copies, waits for them, and re-layouts: 2.62 us -> 1.24 us
where the time goes in v2:
time: 29.2 us; the launch traced here: 29.1 us
  Pallas kernels  27.8 us (95%)
  local copies, waits for them, and re-layouts  1.24 us (4%)
    pallas_call x1, Pallas kernels, shards(): pl.pallas_call(functools.partial(kernel, holders, askers), out_shape=jax....  27.8 us
    unnamed x1, local copies, waits for them, and re-layouts  1.24 us

profile of v2, /device:TPU:0, one launch (start us, length us, event | category | flops | bytes accessed | tf_op | source)
XLA Modules:
  0.0 29.1 jit_solution(9792842413783311617)
XLA Ops:
  0.0 27.8 %shard_map.46 = f32[1,256]{1,0:T(1,128)} custom-call(bf16[1,32,128]{2,1,0:T(8,128)(2,1)} %q_ref.1, s32[1,256]{1,0:T(1,128)} %cand_ref.1, s32[1,512]{1,0:T(1,128)} %bitcast.1, bf16[128,256,128]{2,1,0:T(8,128)(2,1)} %emb_ref.1), custom_call_target="tpu_custom_call" | custom-call | tf_op jit(solution)/shard_map/pallas_call | solution.py:202
  27.8 1.2 %copy.6 = f32[1,256]{1,0:T(1,128)} copy(f32[1,256]{1,0:T(1,128)} %shard_map.46) | data formatting | bytes 2048

commit v3 on v2

--- a/solution.py
+++ b/solution.py
@@ -29,7 +29,7 @@
 def kernel(
     holders, askers, q_ref, cand_ref, slot_ref, emb_ref, out_ref,
     pages, qbuf, best, arrived, row, table, cand, slot,
-    load_sem, own_sem, in_sem, qz_sem, qh_sem, qr_sem, ms_sem, mr_sem, ss_sem, sr_sem,
+    load_sem, own_sem, in_sem, qh_sem, qr_sem, ms_sem, mr_sem, ss_sem, sr_sem,
 ):
     h = lax.axis_index("holder")
     z = lax.axis_index("query")
@@ -39,6 +39,9 @@
     block = count // BLOCKS
     z_peers = [lax.rem(z + d, askers) for d in range(1, askers)]
     h_peers = [lax.rem(h + d, holders) for d in range(1, holders)]
+    middle = askers // 2
+    far = [(dz, dh) for dz in range(askers) for dh in range(holders) if dz or dh]
+    far.sort(key=lambda d: abs(abs(d[0] - middle) - middle))
 
     own = pl.ds(pl.multiple_of(h * tokens, tokens), tokens)
     keep = pltpu.make_async_copy(q_ref.at[0], qbuf.at[z, own], own_sem)
@@ -56,40 +59,80 @@
     def load(b):
         return pltpu.make_async_copy(emb_ref.at[block_of(b)], pages.at[block_of(b)], load_sem.at[b])
 
-    for b in range(BLOCKS):
-        load(b).start()
+    load(0).start()
 
     barrier = pltpu.get_barrier_semaphore()
-    for peer in z_peers:
-        pl.semaphore_signal(barrier, inc=1, device_id={"query": peer}, device_id_type=MESH)
-    for peer in h_peers:
-        pl.semaphore_signal(barrier, inc=1, device_id={"holder": peer}, device_id_type=MESH)
-
-    pl.semaphore_wait(barrier, askers + holders - 2)
+    for dz, dh in far:
+        at, peer = lax.rem(z + dz, askers), lax.rem(h + dh, holders)
+        pl.semaphore_signal(barrier, inc=1, device_id={"holder": peer, "query": at}, device_id_type=MESH)
+    pl.semaphore_wait(barrier, askers * holders - 1)
 
     sends = []
-    for peer in z_peers:
+    for dz, dh in far:
+        at, peer = lax.rem(z + dz, askers), lax.rem(h + dh, holders)
         copy = pltpu.make_async_remote_copy(
-            src_ref=q_ref.at[0], dst_ref=qbuf.at[z, own], send_sem=qz_sem.at[peer],
-            recv_sem=qr_sem.at[z, h], device_id={"query": peer}, device_id_type=MESH,
+            src_ref=q_ref.at[0], dst_ref=qbuf.at[z, own], send_sem=qh_sem.at[at, peer],
+            recv_sem=qr_sem.at[z, h], device_id={"holder": peer, "query": at}, device_id_type=MESH,
         )
         copy.start()
         sends.append(copy)
 
-    def forward(at, src):
-        for peer in h_peers:
-            copy = pltpu.make_async_remote_copy(
-                src_ref=src, dst_ref=qbuf.at[at, own], send_sem=qh_sem.at[at, peer],
-                recv_sem=qr_sem.at[at, h], device_id={"holder": peer}, device_id_type=MESH,
-            )
-            copy.start()
-            sends.append(copy)
+    for b in range(1, BLOCKS):
+        load(b).start()
 
     def await_query(at, who):
         rows = pl.ds(pl.multiple_of(who * tokens, tokens), tokens)
         pltpu.make_async_copy(qbuf.at[at, rows], qbuf.at[at, rows], qr_sem.at[at, who]).wait()
 
-    forward(z, q_ref.at[0])
+    keep.wait()
+
+    together = max(1, WIDE // cols)
+    if askers % together:
+        together = 1
+    rounds = askers // together
+
+    def hand_over(at, b):
+        return pltpu.make_async_remote_copy(
+            src_ref=best.at[at, block_of(b)], dst_ref=arrived.at[z, block_of(b)], send_sem=ms_sem.at[at, b],
+            recv_sem=mr_sem.at[z, b], device_id={"query": at}, device_id_type=MESH,
+        )
+
+    mine = z // together
+    early = BLOCKS // 2
+    order = [(0, 0, early)] + [(i, 0, BLOCKS) for i in range(1, rounds)] + [(0, early, BLOCKS)]
+    for turn, (i, begin, end) in enumerate(order):
+        first = lax.rem(mine + i, rounds) * together
+        if i == 0:
+            members = [first + lax.rem(lax.rem(z, together) + j, together) for j in range(together)]
+            others = members[1:]
+        else:
+            members = [first + j for j in range(together)]
+            others = members
+        if turn == 1:
+            for b in range(early, BLOCKS):
+                load(b).wait()
+        if begin == 0:
+            for at in members:
+                for peer in h_peers:
+                    await_query(at, peer)
+            for at in others:
+                await_query(at, h)
+
+        def work(b, carry):
+            if turn == 0:
+                load(b).wait()
+            part = block_of(b)
+            tall = pages[part].reshape(block * patches, width)
+            tok = qbuf[pl.ds(first, together)].reshape(together * cols, width)
+            sims = dot(tall, tok, NT).reshape(block, patches, together * cols)
+            top = jnp.max(sims, axis=1)
+            for j in range(together):
+                best[first + j, part, :] = top[:, j * cols : (j + 1) * cols]
+            for at in others:
+                hand_over(at, b).start()
+            return carry
+
+        lax.fori_loop(begin, end, work, 0)
 
     for copy in small:
         copy.wait()
@@ -104,52 +147,6 @@
     at_row = place[1:2].astype(jnp.int32)
     row_ids = lax.broadcasted_iota(jnp.int32, (count, wanted.shape[1]), 0)
     is_row = (row_ids == at_row).astype(jnp.float32).astype(jnp.bfloat16)
-
-    keep.wait()
-    for peer in z_peers:
-        await_query(peer, h)
-        forward(peer, qbuf.at[peer, own])
-
-    together = max(1, WIDE // cols)
-    if askers % together:
-        together = 1
-    rounds = askers // together
-
-    def hand_over(at, b):
-        return pltpu.make_async_remote_copy(
-            src_ref=best.at[at, block_of(b)], dst_ref=arrived.at[z, block_of(b)], send_sem=ms_sem.at[at, b],
-            recv_sem=mr_sem.at[z, b], device_id={"query": at}, device_id_type=MESH,
-        )
-
-    mine = z // together
-    for i in range(rounds):
-        chunk = lax.rem(mine + 1 + i, rounds)
-        first = chunk * together
-        if i == rounds - 1:
-            members = [first + lax.rem(lax.rem(z, together) + j, together) for j in range(together)]
-            others = members[1:]
-        else:
-            members = [first + j for j in range(together)]
-            others = members
-        for at in members:
-            for peer in h_peers:
-                await_query(at, peer)
-
-        def work(b, carry):
-            if i == 0:
-                load(b).wait()
-            part = block_of(b)
-            tall = pages[part].reshape(block * patches, width)
-            tok = qbuf[pl.ds(first, together)].reshape(together * cols, width)
-            sims = dot(tall, tok, NT).reshape(block, patches, together * cols)
-            top = jnp.max(sims, axis=1)
-            for j in range(together):
-                best[first + j, part, :] = top[:, j * cols : (j + 1) * cols]
-            for at in others:
-                hand_over(at, b).start()
-            return carry
-
-        lax.fori_loop(0, BLOCKS, work, 0)
 
     parts = []
     for b in range(BLOCKS):
@@ -216,7 +213,6 @@
             dma((BLOCKS,)),
             dma,
             dma((2,)),
-            dma((askers,)),
             dma((askers, holders)),
             dma((askers, holders)),
             dma((askers, BLOCKS)),

time: 29.2 us -> 28.3 us (0.969)
  Pallas kernels: 27.8 us -> 26.9 us
    pallas_call x1, Pallas kernels: 27.8 us -> 26.9 us  [shards(): pl.pallas_call(functools.partial(kernel, holders, askers), out_shape=jax....]
where the time goes in v3:
time: 28.3 us; the launch traced here: 28.1 us
  Pallas kernels  26.9 us (95%)
  local copies, waits for them, and re-layouts  1.24 us (4%)
    pallas_call x1, Pallas kernels, shards(): pl.pallas_call(functools.partial(kernel, holders, askers), out_shape=jax....  26.9 us
    unnamed x1, local copies, waits for them, and re-layouts  1.24 us

profile of v3, /device:TPU:0, one launch (start us, length us, event | category | flops | bytes accessed | tf_op | source)
XLA Modules:
  0.0 28.1 jit_solution(10131424907961376176)
XLA Ops:
  0.0 26.9 %shard_map.46 = f32[1,256]{1,0:T(1,128)} custom-call(bf16[1,32,128]{2,1,0:T(8,128)(2,1)} %q_ref.1, s32[1,256]{1,0:T(1,128)} %cand_ref.1, s32[1,512]{1,0:T(1,128)} %bitcast.1, bf16[128,256,128]{2,1,0:T(8,128)(2,1)} %emb_ref.1), custom_call_target="tpu_custom_call" | custom-call | tf_op jit(solution)/shard_map/pallas_call | solution.py:199
  26.9 1.2 %copy.6 = f32[1,256]{1,0:T(1,128)} copy(f32[1,256]{1,0:T(1,128)} %shard_map.46) | data formatting | bytes 2048
